TPU v7x, 32 devices: a whole 2x2x4 slice. The times are simulated.
32 devices in a mesh: groups: 2 (over y), dom: 16 (over z, x, core).
Axes of the slice: x: 2, y: 2, z: 4, core: 2. Of those that a mesh axis runs over, the one named last changes fastest.
Arguments:
- nodes: bfloat16 [4096, 512], P(('groups', 'dom')), parts along dimension 0, may hold values from -6 to 6
- edges: bfloat16 [24576, 512], P(('groups', 'dom')), parts along dimension 0, may hold values from -6 to 6
- inner_pairs: int32 [8192, 2], P(('groups', 'dom')), parts along dimension 0, may hold values from 0 to 127
- cut_local: int32 [4096], P(('groups', 'dom')), parts along dimension 0, may hold values from 0 to 127
- cut_dest: int32 [4096, 1], P(('groups', 'dom')), parts along dimension 0, may hold values from 0 to 15; in each aligned block of 128 rows (0 to 127, 128 to 255, ...) at most 16 rows name the same one
- cut_remote: int32 [4096], P(('groups', 'dom')), parts along dimension 0, may hold values from 0 to 127
- w_edge_in: bfloat16 [1536, 512], replicated, may hold values from -0.15625 to 0.15625
- w_edge_out: bfloat16 [512, 512], replicated, may hold values from -0.25 to 0.25
- w_node_in: bfloat16 [1024, 512], replicated, may hold values from -0.1875 to 0.1875
- w_node_out: bfloat16 [512, 512], replicated, may hold values from -0.25 to 0.25
- ct_nodes: bfloat16 [4096, 512], P(('groups', 'dom')), parts along dimension 0, may hold values from -6 to 6
- ct_edges: bfloat16 [24576, 512], P(('groups', 'dom')), parts along dimension 0, may hold values from -6 to 6
Outputs:
- new_nodes: bfloat16 [4096, 512], P(('groups', 'dom')), parts along dimension 0
- new_edges: bfloat16 [24576, 512], P(('groups', 'dom')), parts along dimension 0
- grad_nodes: float32 [4096, 512], P(('groups', 'dom')), parts along dimension 0
- grad_edges: float32 [24576, 512], P(('groups', 'dom')), parts along dimension 0
- grad_edge_in: bfloat16 [3072, 512], P('groups'), parts along dimension 0
- grad_edge_out: bfloat16 [1024, 512], P('groups'), parts along dimension 0
- grad_node_in: bfloat16 [2048, 512], P('groups'), parts along dimension 0
- grad_node_out: bfloat16 [1024, 512], P('groups'), parts along dimension 0
There are 2 independent parts, one for each index of `groups`. A program takes and returns all parts, laid end to end along the dimension named above; an argument that names none is the same for every part. Nothing has to cross between parts.
Inputs may be any that keep to these rules, and one draw needn't show every extreme that they name: `cut_dest`: among the cut pairs of one device, at most 16 name any one device, and in every draw some device's pairs name some device exactly 16 times.
All inputs are finite; a program needn't handle non-finite values.
Results may differ from a plain program's by a relative error of at most 0.0085.
Values may be sent and summed in bfloat16 or wider, within the bound.
No kernel may reach another device: no remote copies, remote signals or barrier semaphores. Data moves between devices by JAX's collectives and lax.ppermute only.
A program may use at most 128 MiB of HBM per device.

v0:
```python
import jax
import jax.numpy as jnp
from jax import lax
from jax.sharding import PartitionSpec as P


def layer_norm(values):
    row_mean = jnp.mean(values, axis=-1, keepdims=True)
    centered = values - row_mean
    inv_scale = lax.rsqrt(jnp.mean(centered * centered, axis=-1, keepdims=True) + 1e-05)
    return (centered * inv_scale, inv_scale)


def mlp_forward(inputs, w_first, w_second):
    pre_hidden = jnp.dot(inputs, w_first, preferred_element_type=jnp.float32)
    hidden = jax.nn.silu(pre_hidden).astype(jnp.bfloat16)
    pre_out = jnp.dot(hidden, w_second, preferred_element_type=jnp.float32)
    normed, _ = layer_norm(pre_out)
    return (normed, hidden, pre_hidden, pre_out)


def mlp_backward(inputs, hidden, pre_hidden, pre_out, w_first, w_second, upstream):
    normed, inv_scale = layer_norm(pre_out)
    centered_grad = (
        upstream
        - jnp.mean(upstream, axis=-1, keepdims=True)
        - normed * jnp.mean(upstream * normed, axis=-1, keepdims=True)
    )
    grad_out = (inv_scale * centered_grad).astype(jnp.bfloat16)
    grad_second = lax.dot_general(
        hidden, grad_out, (((0,), (0,)), ((), ())), preferred_element_type=jnp.float32
    )
    grad_hidden = lax.dot_general(
        grad_out, w_second, (((1,), (1,)), ((), ())), preferred_element_type=jnp.float32
    )
    sigmoid_val = jax.nn.sigmoid(pre_hidden)
    grad_pre = (grad_hidden * sigmoid_val * (1.0 + pre_hidden * (1.0 - sigmoid_val))).astype(
        jnp.bfloat16
    )
    grad_first = lax.dot_general(
        inputs, grad_pre, (((0,), (0,)), ((), ())), preferred_element_type=jnp.float32
    )
    grad_inputs = lax.dot_general(
        grad_pre, w_first, (((1,), (1,)), ((), ())), preferred_element_type=jnp.float32
    )
    return (grad_inputs, grad_first, grad_second)


def edge_inputs(edge_rows, first_rows, second_rows):
    latent = first_rows.shape[1]
    senders = jnp.stack([first_rows, second_rows], axis=1).reshape(-1, latent)
    receivers = jnp.stack([second_rows, first_rows], axis=1).reshape(-1, latent)
    return jnp.concatenate([edge_rows, senders, receivers], axis=1)


def agg_targets_order(inner_a, inner_b, cut_local, asked_flat):
    return jnp.concatenate([inner_a, inner_b, cut_local, asked_flat], axis=0)


def shards(
    nodes,
    edges,
    inner_pairs,
    cut_local,
    cut_dest,
    cut_remote,
    w_edge_in,
    w_edge_out,
    w_node_in,
    w_node_out,
    ct_nodes,
    ct_edges,
):
    domains = lax.axis_size("dom")
    node_rows = nodes.shape[0]
    latent = nodes.shape[1]
    inner_count = inner_pairs.shape[0]
    cut_count = cut_local.shape[0]
    slot_count = max(2, 2 * cut_count // domains)
    total_slots = domains * slot_count
    target_dev = cut_dest[:, 0]
    dest_marks = (target_dev[:, None] == jnp.arange(domains, dtype=jnp.int32)[None, :]).astype(
        jnp.int32
    )
    before = jnp.cumsum(dest_marks, axis=0) - dest_marks
    slot_rank = jnp.sum(before * dest_marks, axis=1)
    position = target_dev * slot_count + slot_rank
    slot_node = jnp.zeros((total_slots,), jnp.int32).at[position].set(cut_remote)
    slot_pair = (
        jnp.zeros((total_slots,), jnp.int32)
        .at[position]
        .set(jnp.arange(cut_count, dtype=jnp.int32))
    )
    slot_used = jnp.zeros((total_slots,), jnp.int32).at[position].set(1)
    asked_ids = lax.all_to_all(
        slot_node.reshape(domains, slot_count), "dom", split_axis=0, concat_axis=0, tiled=True
    )
    fetched, asked_ids = (
        lax.all_to_all(nodes[asked_ids], "dom", split_axis=0, concat_axis=0, tiled=True),
        asked_ids,
    )
    asked_flat = asked_ids.reshape(-1)
    far_rows = fetched.reshape(total_slots, latent)[position]
    inner_a = inner_pairs[:, 0]
    inner_b = inner_pairs[:, 1]
    inner_input = edge_inputs(edges[: 2 * inner_count], nodes[inner_a], nodes[inner_b])
    cut_input = edge_inputs(edges[2 * inner_count :], nodes[cut_local], far_rows)
    edge_input = jnp.concatenate([inner_input, cut_input], axis=0)
    edge_out, edge_hidden, edge_pre_hidden, edge_pre_out = mlp_forward(
        edge_input, w_edge_in, w_edge_out
    )
    message = edge_out.astype(jnp.bfloat16)
    new_edges = (edges.astype(jnp.float32) + message.astype(jnp.float32)).astype(jnp.bfloat16)
    message_pairs = message.reshape(inner_count + cut_count, 2, latent)
    outgoing = jnp.where(
        slot_used[:, None] > 0,
        message_pairs[inner_count:, 0][slot_pair],
        jnp.zeros((), jnp.bfloat16),
    )
    incoming = lax.all_to_all(
        outgoing.reshape(domains, slot_count, latent),
        "dom",
        split_axis=0,
        concat_axis=0,
        tiled=True,
    ).reshape(total_slots, latent)
    agg_values = jnp.concatenate(
        [
            message_pairs[:inner_count, 0],
            message_pairs[:inner_count, 1],
            message_pairs[inner_count:, 1],
            incoming,
        ],
        axis=0,
    )
    agg_targets = jnp.concatenate([inner_b, inner_a, cut_local, asked_flat], axis=0)
    onehot = (jnp.arange(node_rows, dtype=jnp.int32)[:, None] == agg_targets[None, :]).astype(
        jnp.bfloat16
    )
    aggregate = jnp.dot(onehot, agg_values, preferred_element_type=jnp.float32).astype(jnp.bfloat16)
    node_input = jnp.concatenate([nodes, aggregate], axis=1)
    node_out, node_hidden, node_pre_hidden, node_pre_out = mlp_forward(
        node_input, w_node_in, w_node_out
    )
    new_nodes = (nodes.astype(jnp.float32) + node_out).astype(jnp.bfloat16)
    ct_node_f = ct_nodes.astype(jnp.float32)
    ct_edge_f = ct_edges.astype(jnp.float32)
    grad_node_input, grad_node_in, grad_node_out = mlp_backward(
        node_input, node_hidden, node_pre_hidden, node_pre_out, w_node_in, w_node_out, ct_node_f
    )
    grad_aggregate = grad_node_input[:, latent:].astype(jnp.bfloat16)
    far_grads = lax.all_to_all(
        grad_aggregate[asked_ids], "dom", split_axis=0, concat_axis=0, tiled=True
    ).reshape(total_slots, latent)[position]
    toward_second = jnp.concatenate([grad_aggregate[inner_b], far_grads], axis=0)
    toward_first = jnp.concatenate([grad_aggregate[inner_a], grad_aggregate[cut_local]], axis=0)
    receiver_grads = jnp.stack([toward_second, toward_first], axis=1).reshape(-1, latent)
    grad_message = ct_edge_f + receiver_grads.astype(jnp.float32)
    grad_edge_input, grad_edge_in, grad_edge_out = mlp_backward(
        edge_input, edge_hidden, edge_pre_hidden, edge_pre_out, w_edge_in, w_edge_out, grad_message
    )
    grad_edge_in, grad_edge_out, grad_node_in, grad_node_out = lax.psum(
        (grad_edge_in, grad_edge_out, grad_node_in, grad_node_out), "dom"
    )
    grad_edges = ct_edge_f + grad_edge_input[:, :latent]
    send_grads = grad_edge_input[:, latent : 2 * latent].reshape(inner_count + cut_count, 2, latent)
    recv_grads = grad_edge_input[:, 2 * latent :].reshape(inner_count + cut_count, 2, latent)
    first_grads = send_grads[:, 0] + recv_grads[:, 1]
    used_rows = slot_used[:, None] > 0
    both_grads = jnp.stack([recv_grads[inner_count:, 0], send_grads[inner_count:, 1]], axis=1)
    outgoing_grads = jnp.where(used_rows[:, :, None], both_grads[slot_pair], 0.0)
    returned_pairs = lax.all_to_all(
        outgoing_grads.reshape(domains, slot_count, 2, latent).astype(jnp.bfloat16),
        "dom",
        split_axis=0,
        concat_axis=0,
        tiled=True,
    ).astype(jnp.float32)
    returned = (returned_pairs[:, :, 0] + returned_pairs[:, :, 1]).reshape(total_slots, latent)
    inner_second_grads = recv_grads[:inner_count, 0] + send_grads[:inner_count, 1]
    grad_values = jnp.concatenate(
        [first_grads[:inner_count], inner_second_grads, first_grads[inner_count:], returned], axis=0
    )
    grad_nodes = (
        ct_node_f
        + grad_node_input[:, :latent]
        + jax.ops.segment_sum(
            grad_values, agg_targets_order(inner_a, inner_b, cut_local, asked_flat), node_rows
        )
    )
    return (
        new_nodes,
        new_edges,
        grad_nodes,
        grad_edges,
        grad_edge_in.astype(jnp.bfloat16),
        grad_edge_out.astype(jnp.bfloat16),
        grad_node_in.astype(jnp.bfloat16),
        grad_node_out.astype(jnp.bfloat16),
    )


def solution(mesh):
    placed = (
        P(("groups", "dom"), None),
        P(("groups", "dom"), None),
        P(("groups", "dom"), None),
        P(("groups", "dom")),
        P(("groups", "dom"), None),
        P(("groups", "dom")),
        P(),
        P(),
        P(),
        P(),
        P(("groups", "dom"), None),
        P(("groups", "dom"), None),
    )
    return jax.shard_map(
        shards,
        mesh=mesh,
        in_specs=placed,
        out_specs=(
            P(("groups", "dom"), None),
            P(("groups", "dom"), None),
            P(("groups", "dom"), None),
            P(("groups", "dom"), None),
            P("groups", None),
            P("groups", None),
            P("groups", None),
            P("groups", None),
        ),
        check_vma=False,
    )
```

profile of v0, /device:TPU:1, one launch (start us, length us, event | category | flops | bytes accessed | tf_op | source)
XLA Modules:
  0.0 327.1 jit_solution(961602621325762036)
XLA Ops:
  3.2 1.1 scatter_custom_fusion
  5.0 7.3 %all-to-all-start = ((s32[16,1,16]{2,1,0:T(1,128)}), s32[16,1,16]{2,1,0:T(1,128)S(1)}, u32[]{:S(2)}, u32[]{:S(2)}) async-start(s32[16,1,16]{2,1,0:T(1,128)} %all_to_all.20), calls=%async_computation | async-start | bytes 16384 | tf_op jit(solution)/shard_map/all_to_all | solution.py:95
  14.4 1.2 gather_fusion.1
  15.5 1.2 gather_fusion
  18.7 1.9 gather_fusion.3
  20.5 6.0 %all-to-all-start.1 = ((bf16[16,16,512]{2,1,0:T(8,128)(2,1)}), bf16[16,16,512]{2,1,0:T(8,128)(2,1)S(1)}, u32[]{:S(2)}, u32[]{:S(2)}) async-start(bf16[16,16,512]{2,1,0:T(8,128)(2,1)} %bitcast.11), calls=%async_computation.1 | async-start | bytes 524288 | tf_op jit(solution)/shard_map/all_to_all | solution.py:99
  29.0 1.6 copy.38
  30.6 1.0 reshape.152
  33.1 1.1 scatter_custom_fusion.2
  38.9 3.9 %multiply_convert_fusion.2 = (bf16[768,512]{1,0:T(8,128)(2,1)S(1)}, f32[768,512]{1,0:T(8,128)}) fusion(bf16[1536,512]{1,0:T(8,128)(2,1)S(1)} %copy-done, bf16[256,512]{1,0:T(8,128)(2,1)S(1)} %reshape.155, bf16[256,512]{1,0:T(8,128)(2,1)S(1)} %reshape.154, bf16[256,512]{1,0:T(8,128)(2,1)} %slice.79, bf16[512,512]{1,0:T(8,128)(2,1)S(1)} %copy-done.20, ...), kind=kOutput, calls=%fused_computation.32 | convolution fusion | flops 1224081408 | bytes 6291456 | tf_op jit(solution)/shard_map/dot_general | solution.py:15
  44.2 1.5 add_convert_fusion
  45.7 2.8 reshape.156
  48.6 2.2 fusion.47
  50.8 2.0 gather_fusion.5
  52.8 1.8 broadcast_select_fusion
  54.5 6.0 %all-to-all-start.2 = ((bf16[16,16,512]{2,1,0:T(8,128)(2,1)}), bf16[16,16,512]{2,1,0:T(8,128)(2,1)S(1)}, u32[]{:S(2)}, u32[]{:S(2)}) async-start(bf16[16,16,512]{2,1,0:T(8,128)(2,1)} %broadcast_select_fusion), calls=%async_computation.2 | async-start | bytes 524288 | tf_op jit(solution)/shard_map/all_to_all | solution.py:120
  60.5 1.6 copy.73
  62.2 2.3 fusion.46
  65.4 4.6 %all-to-all-done.2 = bf16[16,16,512]{2,1,0:T(8,128)(2,1)S(1)} async-done(((bf16[16,16,512]{2,1,0:T(8,128)(2,1)}), bf16[16,16,512]{2,1,0:T(8,128)(2,1)S(1)}, u32[]{:S(2)}, u32[]{:S(2)}) %all-to-all-start.2) | async-done | bytes 262176 | tf_op jit(solution)/shard_map/all_to_all | solution.py:120
  70.0 1.5 convolution_convert_fusion
  75.9 1.8 fusion.26
  77.8 1.9 gather_fusion.7
  79.6 4.3 %all-to-all-start.3 = ((bf16[16,16,512]{2,1,0:T(8,128)(2,1)}), bf16[16,16,512]{2,1,0:T(8,128)(2,1)S(1)}, u32[]{:S(2)}, u32[]{:S(2)}) async-start(bf16[16,16,512]{2,1,0:T(8,128)(2,1)} %bitcast.67), calls=%async_computation.3 | async-start | bytes 524288 | tf_op jit(solution)/shard_map/all_to_all | solution.py:152
  83.9 2.5 fusion.39
  86.4 1.6 gather_fusion.10
  88.0 2.0 gather_fusion.9
  90.0 2.0 gather_fusion.6
  92.0 1.8 maximum_bitcast_fusion.1
  93.8 1.8 convert_add_fusion.2
  97.5 1.1 maximum_convert_fusion
  98.6 2.4 copy.45
  101.0 3.2 reshape.161
  104.1 2.4 fusion.19
  110.1 1.4 fusion.52
  111.5 2.3 convert_add_fusion
  113.8 2.2 reshape.160
  116.3 1.7 slice.134
  117.9 3.4 %reshape.159 = f32[384,2,512]{2,1,0:T(2,128)} reshape(f32[768,512]{1,0:T(8,128)} %get-tuple-element.20) | data formatting | bytes 3145728 | tf_op jit(solution)/shard_map/reshape | solution.py:166
  121.3 1.4 slice.140
  122.9 1.4 slice.137
  124.3 1.2 slice.136
  127.5 14.0 %fusion.43 = f32[1536,512]{1,0:T(8,128)} fusion(bf16[768,512]{1,0:T(8,128)(2,1)S(1)} %copy-done.40, bf16[256,512]{1,0:T(8,128)(2,1)S(1)} %copy-done.27, bf16[256,512]{1,0:T(8,128)(2,1)S(1)} %copy-done.29, bf16[256,512]{1,0:T(8,128)(2,1)S(1)} %copy-done.25, bf16[512,512]{1,0:T(8,128)(2,1)S(1)} %copy-done.21, bf16[512,512]{1,0:T(8,128)(2,1)S(1)} %copy-done.22, ...), kind=kOutput, calls=%fused_computation.129 | convolution fusion | flops 1222115328 | bytes 6291456 | tf_op jit(solution)/shard_map/dot_general | solution.py:40
  142.7 1.9 gather_fusion.11
  145.6 6.1 %all-to-all-start.4 = ((bf16[16,16,2,512]{3,1,2,0:T(8,128)(2,1)}), bf16[16,16,2,512]{3,1,2,0:T(8,128)(2,1)}, u32[]{:S(2)}, u32[]{:S(2)}) async-start(bf16[16,16,2,512]{3,1,2,0:T(8,128)(2,1)} %fusion.11), calls=%async_computation.4 | async-start | bytes 1048576 | tf_op jit(solution)/shard_map/all_to_all | solution.py:172
  151.6 1.3 fusion.20
  152.9 163.8 %all-reduce.2 = (bf16[1536,512]{1,0:T(8,128)(2,1)}, bf16[512,512]{1,0:T(8,128)(2,1)}, bf16[1024,512]{1,0:T(8,128)(2,1)}, bf16[512,512]{1,0:T(8,128)(2,1)}) all-reduce(f32[1536,512]{1,0:T(8,128)} %fusion.43, f32[512,512]{1,0:T(8,128)S(1)} %fusion.53, f32[1024,512]{1,0:T(8,128)} %fusion.26, ...), channel_id=1, replica_groups=mesh['groups'=2,'dom'=16] {'dom'}, use_global_device_ids=true, to_apply=%region_14.15 | all-reduce | flops 1835008 | bytes 11010048 | tf_op jit(solution)/shard_map/psum | solution.py:162
  316.7 1.2 convert_element_type.93
  318.0 8.9 %scatter_custom_fusion.3 = f32[128,512]{1,0:T(8,128)} fusion(f32[128,512]{1,0:T(8,128)} %convert_add_fusion.2, s32[896]{0:T(1024)} %get-tuple-element.30, f32[256,512]{1,0:T(8,128)S(1)} %bitcast.65, f32[]{:T(128)} %constant.48, f32[128,512]{1,0:T(8,128)S(1)} %copy-done.15, f32[256,512]{1,0:T(8,128)S(1)} %fusion.20, f32[256,512]{1,0:T(8,128)S(1)} %copy-done.13), kind=kCustom, calls=%fused_computation.19 | custom fusion | flops 1835008 | bytes 2097664 | tf_op jit(solution)/shard_map/scatter-add | solution.py:187
  (162 shorter events, 32.2 us)
Async XLA Ops:
  0.6 37.9 %copy-start = (bf16[1536,512]{1,0:T(8,128)(2,1)S(1)}, bf16[1536,512]{1,0:T(8,128)(2,1)}, u32[]{:S(2)}) copy-start(bf16[1536,512]{1,0:T(8,128)(2,1)} %param.18) | copy-start | bytes 4718596
  0.6 13.7 %copy-start.1 = (bf16[128,512]{1,0:T(8,128)(2,1)S(1)}, bf16[128,512]{1,0:T(8,128)(2,1)}, u32[]{:S(2)}) copy-start(bf16[128,512]{1,0:T(8,128)(2,1)} %param.12) | copy-start | bytes 393220
  5.0 13.6 %all-to-all-start = ((s32[16,1,16]{2,1,0:T(1,128)}), s32[16,1,16]{2,1,0:T(1,128)S(1)}, u32[]{:S(2)}, u32[]{:S(2)}) async-start(s32[16,1,16]{2,1,0:T(1,128)} %all_to_all.20), calls=%async_computation | async-start | bytes 16384 | tf_op jit(solution)/shard_map/all_to_all | solution.py:95
  13.8 0.6 copy-start.31
  14.3 2.3 copy-start.32
  18.6 8.0 %copy-start.11 = (bf16[768,512]{1,0:T(8,128)(2,1)S(1)}, bf16[768,512]{1,0:T(8,128)(2,1)}, u32[]{:S(2)}) copy-start(bf16[768,512]{1,0:T(8,128)(2,1)} %param.13) | copy-start | bytes 2359300
  18.6 18.3 %copy-start.33 = (s32[1024]{0:T(1024)}, s32[1024]{0:T(1024)S(1)}, u32[]{:S(2)}) copy-start(s32[1024]{0:T(1024)S(1)} %pad_clamp_fusion.1) | copy-start | bytes 12292
  20.5 16.3 %all-to-all-start.1 = ((bf16[16,16,512]{2,1,0:T(8,128)(2,1)}), bf16[16,16,512]{2,1,0:T(8,128)(2,1)S(1)}, u32[]{:S(2)}, u32[]{:S(2)}) async-start(bf16[16,16,512]{2,1,0:T(8,128)(2,1)} %bitcast.11), calls=%async_computation.1 | async-start | bytes 524288 | tf_op jit(solution)/shard_map/all_to_all | solution.py:99
  26.6 4.0 %copy-start.34 = (s32[1024]{0:T(1024)}, s32[1024]{0:T(1024)S(1)}, u32[]{:S(2)}) copy-start(s32[1024]{0:T(1024)S(1)} %pad_clamp_fusion.3) | copy-start | bytes 12292
  30.6 5.6 %copy-start.37 = (s32[128]{0:T(128)S(1)}, s32[128]{0:T(128)}, u32[]{:S(2)}) copy-start(s32[128]{0:T(128)} %param.15) | copy-start | bytes 1540
  37.7 1.0 copy-start.18
  37.7 1.2 copy-start.20
  38.1 4.6 %copy-start.26 = (bf16[256,512]{1,0:T(8,128)(2,1)}, bf16[256,512]{1,0:T(8,128)(2,1)S(1)}, u32[]{:S(2)}) copy-start(bf16[256,512]{1,0:T(8,128)(2,1)S(1)} %reshape.155) | copy-start | bytes 786436
  38.9 3.9 %copy-start.28 = (bf16[256,512]{1,0:T(8,128)(2,1)}, bf16[256,512]{1,0:T(8,128)(2,1)S(1)}, u32[]{:S(2)}) copy-start(bf16[256,512]{1,0:T(8,128)(2,1)S(1)} %reshape.154) | copy-start | bytes 786436
  38.9 3.9 %copy-start.23 = (bf16[512,512]{1,0:T(8,128)(2,1)S(1)}, bf16[512,512]{1,0:T(8,128)(2,1)}, u32[]{:S(2)}) copy-start(bf16[512,512]{1,0:T(8,128)(2,1)} %param.19) | copy-start | bytes 1572868
  42.8 1.0 copy-start.9
  42.8 1.4 copy-start.12
  54.5 15.5 %all-to-all-start.2 = ((bf16[16,16,512]{2,1,0:T(8,128)(2,1)}), bf16[16,16,512]{2,1,0:T(8,128)(2,1)S(1)}, u32[]{:S(2)}, u32[]{:S(2)}) async-start(bf16[16,16,512]{2,1,0:T(8,128)(2,1)} %broadcast_select_fusion), calls=%async_computation.2 | async-start | bytes 524288 | tf_op jit(solution)/shard_map/all_to_all | solution.py:120
  70.0 1.5 copy-start.5
  71.5 1.0 copy-start.38
  71.5 1.6 copy-start.17
  72.6 1.4 copy-start.30
  72.9 1.1 copy-start.16
  72.9 1.0 copy-start.35
  73.1 0.8 copy-start.36
  75.9 1.9 copy-start.14
  79.6 15.9 %all-to-all-start.3 = ((bf16[16,16,512]{2,1,0:T(8,128)(2,1)}), bf16[16,16,512]{2,1,0:T(8,128)(2,1)S(1)}, u32[]{:S(2)}, u32[]{:S(2)}) async-start(bf16[16,16,512]{2,1,0:T(8,128)(2,1)} %bitcast.67), calls=%async_computation.3 | async-start | bytes 524288 | tf_op jit(solution)/shard_map/all_to_all | solution.py:152
  104.1 2.4 copy-start.2
  104.1 2.4 copy-start.3
  106.6 1.0 copy-start.24
  106.6 1.7 copy-start.43
  107.2 2.1 copy-start.6
  109.2 0.9 copy-start.39
  121.3 1.6 copy-start.4
  122.8 2.7 slice-start
  122.8 2.7 copy-start.8
  125.5 1.9 copy-start.19
  125.5 1.9 copy-start.21
  125.5 1.9 copy-start.22
  125.5 1.8 copy-start.25
  125.5 1.8 copy-start.27
  125.5 1.8 copy-start.29
  125.5 2.0 copy-start.40
  127.5 14.0 %copy-start.7 = (bf16[768,512]{1,0:T(8,128)(2,1)S(1)}, bf16[768,512]{1,0:T(8,128)(2,1)}, u32[]{:S(2)}) copy-start(bf16[768,512]{1,0:T(8,128)(2,1)} %copy-done.6) | copy-start | bytes 2359300
  127.5 14.0 %copy-start.10 = (bf16[768,512]{1,0:T(8,128)(2,1)S(1)}, bf16[768,512]{1,0:T(8,128)(2,1)}, u32[]{:S(2)}) copy-start(bf16[768,512]{1,0:T(8,128)(2,1)} %copy-done.9) | copy-start | bytes 2359300
  145.6 171.1 %all-to-all-start.4 = ((bf16[16,16,2,512]{3,1,2,0:T(8,128)(2,1)}), bf16[16,16,2,512]{3,1,2,0:T(8,128)(2,1)}, u32[]{:S(2)}, u32[]{:S(2)}) async-start(bf16[16,16,2,512]{3,1,2,0:T(8,128)(2,1)} %fusion.11), calls=%async_computation.4 | async-start | bytes 1048576 | tf_op jit(solution)/shard_map/all_to_all | solution.py:172
  316.7 1.3 copy-start.13
  316.7 1.3 copy-start.15
  (2 other events, 1.1 us)
where the time goes:
time: 334 us; the launch traced here: 327 us
  blocking collectives  164 us (49%)
  local copies, waits for them, and re-layouts  63.3 us (19%)
  other arithmetic  35.4 us (11%)
  starting transfers between devices  29.7 us (9%)
  matrix products  28.7 us (9%)
  waiting for transfers between devices  4.66 us (1%)
    psum x1, blocking collectives, shards(): lax.psum((grad_edge_in, grad_edge_out, grad_node_in, grad_node_out), 'dom')  164 us
    dot_general x2, matrix products, mlp_backward(): lax.dot_general(inputs, grad_pre, (((0,), (0,)), ((), ())), preferred_ele...  15.8 us
    scatter-add x1, other arithmetic, shards(): jax.ops.segment_sum(grad_values, agg_targets_order(inner_a, inner_b, cut_...  8.86 us
    all_to_all x1, starting transfers between devices, shards(): lax.all_to_all(slot_node.reshape(domains, slot_count), 'dom', split_axis=...  7.32 us
    unnamed x90, local copies, waits for them, and re-layouts  7.15 us
  transfers between devices with their start and end apart: 5, of which 1 were waited for; matrix products, arithmetic and copies ran while one was open for 10% of the time, Pallas kernels for 0%

commit v1 on v0

--- a/solution.py
+++ b/solution.py
@@ -159,9 +159,18 @@
     grad_edge_input, grad_edge_in, grad_edge_out = mlp_backward(
         edge_input, edge_hidden, edge_pre_hidden, edge_pre_out, w_edge_in, w_edge_out, grad_message
     )
-    grad_edge_in, grad_edge_out, grad_node_in, grad_node_out = lax.psum(
-        (grad_edge_in, grad_edge_out, grad_node_in, grad_node_out), "dom"
-    )
+    node_total = lax.psum(
+        jnp.concatenate([grad_node_in, grad_node_out], axis=0).astype(jnp.bfloat16), "dom"
+    )
+    edge_part = lax.psum_scatter(
+        jnp.concatenate([grad_edge_in, grad_edge_out], axis=0).astype(jnp.bfloat16),
+        "dom",
+        scatter_dimension=0,
+        tiled=True,
+    )
+    edge_total = lax.all_gather(edge_part, "dom", axis=0, tiled=True)
+    grad_edge_in, grad_edge_out = edge_total[: 3 * latent], edge_total[3 * latent :]
+    grad_node_in, grad_node_out = node_total[: 2 * latent], node_total[2 * latent :]
     grad_edges = ct_edge_f + grad_edge_input[:, :latent]
     send_grads = grad_edge_input[:, latent : 2 * latent].reshape(inner_count + cut_count, 2, latent)
     recv_grads = grad_edge_input[:, 2 * latent :].reshape(inner_count + cut_count, 2, latent)

time: 334 us -> 351 us (1.051)
  blocking collectives: 164 us -> 0 us
  waiting for transfers between devices: 4.66 us -> 156 us
  local copies, waits for them, and re-layouts: 63.3 us -> 78.8 us
  between operations: 1.58 us -> 14.8 us
    psum x1 -> x0, blocking collectives: 164 us -> none  [shards(): lax.psum((grad_edge_in, grad_edge_out, grad_node_in, grad_node_out), 'dom')]
    psum x0 -> x1, waiting for transfers between devices: none -> 63.9 us  [shards(): lax.psum(jnp.concatenate([grad_node_in, grad_node_out], axis=0).astype(jn...]
    reduce_scatter x0 -> x1, waiting for transfers between devices: none -> 54.6 us  [shards(): lax.psum_scatter(jnp.concatenate([grad_edge_in, grad_edge_out], axis=0).a...]
    all_gather x0 -> x1, waiting for transfers between devices: none -> 28.8 us  [shards(): edge_total = lax.all_gather(edge_part, 'dom', axis=0, tiled=True)]
    slice x0 -> x4, local copies, waits for them, and re-layouts: none -> 8.65 us  [the longest x1 2.65 us: shards(): edge_total[:3 * latent]]
    unnamed x90 -> x112, local copies, waits for them, and re-layouts: 7.15 us -> 7.68 us
  transfers between devices with their start and end apart: 5 -> 8, of which waited for: 1 -> 5; matrix products, arithmetic and copies ran while one was open for 10% -> 21% of each run, Pallas kernels for 0% -> 0%
where the time goes in v1:
time: 351 us; the launch traced here: 345 us
  waiting for transfers between devices  156 us (44%)
  local copies, waits for them, and re-layouts  78.8 us (22%)
  other arithmetic  38 us (11%)
  starting transfers between devices  31.1 us (9%)
  matrix products  26.3 us (7%)
  between operations  14.8 us (4%)
    psum x1, waiting for transfers between devices, shards(): lax.psum(jnp.concatenate([grad_node_in, grad_node_out], axis=0).astype(jn...  63.9 us
    reduce_scatter x1, waiting for transfers between devices, shards(): lax.psum_scatter(jnp.concatenate([grad_edge_in, grad_edge_out], axis=0).a...  54.6 us
    all_gather x1, waiting for transfers between devices, shards(): edge_total = lax.all_gather(edge_part, 'dom', axis=0, tiled=True)  28.8 us
    dot_general x2, matrix products, mlp_backward(): lax.dot_general(inputs, grad_pre, (((0,), (0,)), ((), ())), preferred_ele...  13.3 us
    scatter-add x1, other arithmetic, shards(): jax.ops.segment_sum(grad_values, agg_targets_order(inner_a, inner_b, cut_...  9.15 us
    unnamed x112, local copies, waits for them, and re-layouts  7.68 us
    all_to_all x1, starting transfers between devices, shards(): lax.all_to_all(slot_node.reshape(domains, slot_count), 'dom', split_axis=...  7.32 us
  transfers between devices with their start and end apart: 8, of which 5 were waited for; matrix products, arithmetic and copies ran while one was open for 21% of the time, Pallas kernels for 0%

profile of v1, /device:TPU:1, one launch (start us, length us, event | category | flops | bytes accessed | tf_op | source)
XLA Modules:
  0.0 344.6 jit_solution(13716603735672538509)
XLA Ops:
  11.6 7.3 %all-to-all-start = ((s32[16,1,16]{2,1,0:T(1,128)}), s32[16,1,16]{2,1,0:T(1,128)S(1)}, u32[]{:S(2)}, u32[]{:S(2)}) async-start(s32[16,1,16]{2,1,0:T(1,128)} %all_to_all.20), calls=%async_computation | async-start | bytes 16384 | tf_op jit(solution)/shard_map/all_to_all | solution.py:95
  24.7 1.9 gather_fusion.3
  26.5 6.0 %all-to-all-start.1 = ((bf16[16,16,512]{2,1,0:T(8,128)(2,1)}), bf16[16,16,512]{2,1,0:T(8,128)(2,1)S(1)}, u32[]{:S(2)}, u32[]{:S(2)}) async-start(bf16[16,16,512]{2,1,0:T(8,128)(2,1)} %bitcast.11), calls=%async_computation.1 | async-start | bytes 524288 | tf_op jit(solution)/shard_map/all_to_all | solution.py:99
  36.2 1.6 copy.37
  44.8 4.0 %multiply_convert_fusion.2 = (bf16[768,512]{1,0:T(8,128)(2,1)S(1)}, f32[768,512]{1,0:T(8,128)}) fusion(bf16[1536,512]{1,0:T(8,128)(2,1)S(1)} %copy-done, bf16[256,512]{1,0:T(8,128)(2,1)S(1)} %reshape.155, bf16[256,512]{1,0:T(8,128)(2,1)S(1)} %reshape.154, bf16[256,512]{1,0:T(8,128)(2,1)S(1)} %copy-done.32, bf16[512,512]{1,0:T(8,128)(2,1)} %reshape.152, ...), kind=kOutput, calls=%fused_computation.35 | convolution fusion | flops 1224081408 | bytes 6291456 | tf_op jit(solution)/shard_map/dot_general | solution.py:15
  50.2 1.5 add_convert_fusion
  51.7 2.8 reshape.156
  54.6 1.5 fusion.44
  56.7 2.0 gather_fusion.5
  58.7 1.8 broadcast_select_fusion
  60.5 6.0 %all-to-all-start.2 = ((bf16[16,16,512]{2,1,0:T(8,128)(2,1)}), bf16[16,16,512]{2,1,0:T(8,128)(2,1)S(1)}, u32[]{:S(2)}, u32[]{:S(2)}) async-start(bf16[16,16,512]{2,1,0:T(8,128)(2,1)} %broadcast_select_fusion), calls=%async_computation.2 | async-start | bytes 524288 | tf_op jit(solution)/shard_map/all_to_all | solution.py:120
  66.5 2.3 fusion.43
  69.7 6.3 %all-to-all-done.2 = bf16[16,16,512]{2,1,0:T(8,128)(2,1)S(1)} async-done(((bf16[16,16,512]{2,1,0:T(8,128)(2,1)}), bf16[16,16,512]{2,1,0:T(8,128)(2,1)S(1)}, u32[]{:S(2)}, u32[]{:S(2)}) %all-to-all-start.2) | async-done | bytes 262176 | tf_op jit(solution)/shard_map/all_to_all | solution.py:120
  76.0 1.5 convolution_convert_fusion.4
  82.9 1.9 gather_fusion.7
  84.8 4.6 %all-to-all-start.3 = ((bf16[16,16,512]{2,1,0:T(8,128)(2,1)}), bf16[16,16,512]{2,1,0:T(8,128)(2,1)}, u32[]{:S(2)}, u32[]{:S(2)}) async-start(bf16[16,16,512]{2,1,0:T(8,128)(2,1)} %bitcast.69), calls=%async_computation.3 | async-start | bytes 524288 | tf_op jit(solution)/shard_map/all_to_all | solution.py:152
  89.6 1.6 gather_fusion.10
  91.2 2.0 gather_fusion.9
  93.2 2.0 gather_fusion.6
  95.2 1.8 maximum_bitcast_fusion.1
  97.0 1.9 all-to-all-done.3
  99.0 2.6 gather_fusion.8
  103.7 2.4 copy.45
  106.0 3.1 reshape.161
  109.2 2.4 fusion.19
  115.9 12.9 %convolution_convert_fusion = bf16[1536,512]{1,0:T(8,128)(2,1)S(1)} fusion(bf16[768,512]{1,0:T(8,128)(2,1)S(1)} %multiply_convert_fusion, bf16[256,512]{1,0:T(8,128)(2,1)S(1)} %copy-done.37, bf16[256,512]{1,0:T(8,128)(2,1)S(1)} %copy-done.35, bf16[256,512]{1,0:T(8,128)(2,1)S(1)} %copy-done.33, bf16[512,512]{1,0:T(8,128)(2,1)S(1)} %copy-done.25, ...), kind=kOutput, calls=%fused_computation.16 | convolution fusion | flops 1222901760 | bytes 4718592 | tf_op jit(solution)/shard_map/dot_general | solution.py:40
  128.8 1.5 pad_maximum_fusion
  131.8 1.4 convolution_convert_fusion.3
  134.9 54.6 %reduce-scatter.2.cloned.1.call-done = bf16[128,512]{1,0:T(8,128)(2,1)} async-done(((bf16[2048,512]{1,0:T(8,128)(2,1)}), bf16[128,512]{1,0:T(8,128)(2,1)}) %reduce-scatter.2.cloned.1.call-update) | async-done | bytes 131088 | tf_op jit(solution)/shard_map/reduce_scatter | solution.py:165
  190.3 2.6 fusion.49
  192.9 2.3 convert_add_fusion
  195.2 3.1 reshape.160
  198.3 2.0 slice.155
  200.4 2.4 slice.152
  202.8 3.1 slice.150
  205.9 2.1 reshape.159
  208.0 1.4 slice.156
  209.4 2.6 slice.153
  212.6 2.8 gather_fusion.11
  215.4 2.0 fusion.11
  217.4 6.4 %all-to-all-start.4 = ((bf16[16,16,2,512]{3,1,2,0:T(8,128)(2,1)}), bf16[16,16,2,512]{3,1,2,0:T(8,128)(2,1)}, u32[]{:S(2)}, u32[]{:S(2)}) async-start(bf16[16,16,2,512]{3,1,2,0:T(8,128)(2,1)} %fusion.11), calls=%async_computation.4 | async-start | bytes 1048576 | tf_op jit(solution)/shard_map/all_to_all | solution.py:181
  225.3 63.9 %all-reduce.2.cloned.1.call-done = bf16[1536,512]{1,0:T(8,128)(2,1)} async-done(((bf16[1536,512]{1,0:T(8,128)(2,1)}), bf16[1536,512]{1,0:T(8,128)(2,1)}) %all-reduce.2.cloned.1.call-update) | async-done | bytes 1572880 | tf_op jit(solution)/shard_map/psum | solution.py:162
  289.2 1.9 slice.163
  291.1 2.3 slice.162
  295.4 9.1 %scatter_custom_fusion.3 = f32[128,512]{1,0:T(8,128)} fusion(f32[128,512]{1,0:T(8,128)} %convert_add_fusion.2, s32[896]{0:T(1024)} %get-tuple-element.26, f32[256,512]{1,0:T(8,128)} %bitcast.67, f32[]{:T(128)} %constant.50, f32[128,512]{1,0:T(8,128)S(1)} %slice_bitcast_fusion.1, f32[256,512]{1,0:T(8,128)S(1)} %fusion.20, f32[256,512]{1,0:T(8,128)} %slice_bitcast_fusion), kind=kCustom, calls=%fused_computation.21 | custom fusion | flops 1835008 | bytes 2097664 | tf_op jit(solution)/shard_map/scatter-add | solution.py:196
  304.5 28.8 %all-gather.2.cloned.1.call-done = bf16[2048,512]{1,0:T(8,128)(2,1)} async-done(((bf16[128,512]{1,0:T(8,128)(2,1)}), bf16[2048,512]{1,0:T(8,128)(2,1)}) %all-gather.2.cloned.1.call-update) | async-done | bytes 2097168 | tf_op jit(solution)/shard_map/all_gather | solution.py:171
  333.4 1.9 slice.161
  335.2 2.7 slice.160
  (198 shorter events, 43.4 us)
Async XLA Ops:
  7.2 37.4 %copy-start = (bf16[1536,512]{1,0:T(8,128)(2,1)S(1)}, bf16[1536,512]{1,0:T(8,128)(2,1)}, u32[]{:S(2)}) copy-start(bf16[1536,512]{1,0:T(8,128)(2,1)} %param.18) | copy-start | bytes 4718596
  7.2 14.2 %copy-start.1 = (bf16[128,512]{1,0:T(8,128)(2,1)S(1)}, bf16[128,512]{1,0:T(8,128)(2,1)}, u32[]{:S(2)}) copy-start(bf16[128,512]{1,0:T(8,128)(2,1)} %param.12) | copy-start | bytes 393220
  11.6 13.0 %all-to-all-start = ((s32[16,1,16]{2,1,0:T(1,128)}), s32[16,1,16]{2,1,0:T(1,128)S(1)}, u32[]{:S(2)}, u32[]{:S(2)}) async-start(s32[16,1,16]{2,1,0:T(1,128)} %all_to_all.20), calls=%async_computation | async-start | bytes 16384 | tf_op jit(solution)/shard_map/all_to_all | solution.py:95
  20.3 3.4 copy-start.39
  20.3 3.3 copy-start.40
  24.6 8.0 %copy-start.8 = (bf16[768,512]{1,0:T(8,128)(2,1)S(1)}, bf16[768,512]{1,0:T(8,128)(2,1)}, u32[]{:S(2)}) copy-start(bf16[768,512]{1,0:T(8,128)(2,1)} %param.13) | copy-start | bytes 2359300
  24.6 18.3 %copy-start.41 = (s32[1024]{0:T(1024)}, s32[1024]{0:T(1024)S(1)}, u32[]{:S(2)}) copy-start(s32[1024]{0:T(1024)S(1)} %pad_clamp_fusion.1) | copy-start | bytes 12292
  26.5 16.3 %all-to-all-start.1 = ((bf16[16,16,512]{2,1,0:T(8,128)(2,1)}), bf16[16,16,512]{2,1,0:T(8,128)(2,1)S(1)}, u32[]{:S(2)}, u32[]{:S(2)}) async-start(bf16[16,16,512]{2,1,0:T(8,128)(2,1)} %bitcast.11), calls=%async_computation.1 | async-start | bytes 524288 | tf_op jit(solution)/shard_map/all_to_all | solution.py:99
  32.6 5.3 %copy-start.42 = (s32[1024]{0:T(1024)}, s32[1024]{0:T(1024)S(1)}, u32[]{:S(2)}) copy-start(s32[1024]{0:T(1024)S(1)} %pad_clamp_fusion.3) | copy-start | bytes 12292
  37.8 4.4 %copy-start.47 = (s32[128]{0:T(128)S(1)}, s32[128]{0:T(128)}, u32[]{:S(2)}) copy-start(s32[128]{0:T(128)} %param.15) | copy-start | bytes 1540
  44.2 4.6 %copy-start.34 = (bf16[256,512]{1,0:T(8,128)(2,1)}, bf16[256,512]{1,0:T(8,128)(2,1)S(1)}, u32[]{:S(2)}) copy-start(bf16[256,512]{1,0:T(8,128)(2,1)S(1)} %reshape.154) | copy-start | bytes 786436
  44.8 4.0 %copy-start.36 = (bf16[256,512]{1,0:T(8,128)(2,1)}, bf16[256,512]{1,0:T(8,128)(2,1)S(1)}, u32[]{:S(2)}) copy-start(bf16[256,512]{1,0:T(8,128)(2,1)S(1)} %reshape.155) | copy-start | bytes 786436
  44.8 4.0 %copy-start.26 = (bf16[512,512]{1,0:T(8,128)(2,1)S(1)}, bf16[512,512]{1,0:T(8,128)(2,1)}, u32[]{:S(2)}) copy-start(bf16[512,512]{1,0:T(8,128)(2,1)} %param.19) | copy-start | bytes 1572868
  48.8 1.4 copy-start.9
  60.5 15.5 %all-to-all-start.2 = ((bf16[16,16,512]{2,1,0:T(8,128)(2,1)}), bf16[16,16,512]{2,1,0:T(8,128)(2,1)S(1)}, u32[]{:S(2)}, u32[]{:S(2)}) async-start(bf16[16,16,512]{2,1,0:T(8,128)(2,1)} %broadcast_select_fusion), calls=%async_computation.2 | async-start | bytes 524288 | tf_op jit(solution)/shard_map/all_to_all | solution.py:120
  76.0 1.5 copy-start.6
  77.5 1.4 copy-start.28
  77.6 1.6 copy-start.20
  78.6 1.4 copy-start.38
  84.8 14.2 %all-to-all-start.3 = ((bf16[16,16,512]{2,1,0:T(8,128)(2,1)}), bf16[16,16,512]{2,1,0:T(8,128)(2,1)}, u32[]{:S(2)}, u32[]{:S(2)}) async-start(bf16[16,16,512]{2,1,0:T(8,128)(2,1)} %bitcast.69), calls=%async_computation.3 | async-start | bytes 524288 | tf_op jit(solution)/shard_map/all_to_all | solution.py:152
  89.3 100.2 %reduce-scatter.2.cloned.1.call-start = ((), (), s32[]{:S(2)}) async-start(), calls=%async_computation.6 | async-start | bytes 2228224 | tf_op jit(solution)/shard_map/reduce_scatter | solution.py:165
  95.2 6.4 %copy-start.14 = (bf16[256,512]{1,0:T(8,128)(2,1)S(1)}, bf16[256,512]{1,0:T(8,128)(2,1)}, u32[]{:S(2)}) copy-start(bf16[256,512]{1,0:T(8,128)(2,1)} %gather_fusion.6) | copy-start | bytes 786436
  109.2 2.4 copy-start.2
  109.2 2.4 copy-start.3
  111.6 1.1 copy-start.19
  112.8 1.6 copy-start.54
  114.3 1.2 copy-start.24
  114.3 1.4 copy-start.25
  114.3 1.4 copy-start.33
  114.3 1.5 copy-start.35
  114.4 1.6 copy-start.37
  115.9 12.9 %copy-start.49 = (bf16[768,512]{1,0:T(8,128)(2,1)}, bf16[768,512]{1,0:T(8,128)(2,1)S(1)}, u32[]{:S(2)}) copy-start(bf16[768,512]{1,0:T(8,128)(2,1)S(1)} %multiply_convert_fusion) | copy-start | bytes 2359300
  130.3 1.4 copy-start.17
  130.3 1.4 copy-start.21
  130.3 1.4 copy-start.44
  130.3 1.4 copy-start.46
  130.4 1.4 copy-start.51
  130.4 1.4 copy-start.53
  130.4 158.8 %all-reduce.2.cloned.1.call-start = ((), (), s32[]{:S(2)}) async-start(), calls=%async_computation.8 | async-start | bytes 3145728 | tf_op jit(solution)/shard_map/psum | solution.py:162
  134.5 55.1 %copy-start.13 = (f32[128,1024]{1,0:T(8,128)S(1)}, f32[128,1024]{1,0:T(8,128)}, u32[]{:S(2)}) copy-start(f32[128,1024]{1,0:T(8,128)} %copy-done.12) | copy-start | bytes 1572868
  134.5 198.9 %all-gather.2.cloned.1.call-start = ((), (), s32[]{:S(2)}) async-start(), calls=%async_computation.7 | async-start | bytes 2228224 | tf_op jit(solution)/shard_map/all_gather | solution.py:171
  190.3 2.6 copy-start.4
  198.3 7.6 %copy-start.5 = (f32[768,512]{1,0:T(8,128)S(1)}, f32[768,512]{1,0:T(8,128)}, u32[]{:S(2)}) copy-start(f32[768,512]{1,0:T(8,128)} %get-tuple-element.16) | copy-start | bytes 4718596
  208.0 4.0 %copy-start.15 = (bf16[128,1,512]{2,1,0:T(2,128)(2,1)S(1)}, bf16[128,1,512]{2,1,0:T(2,128)(2,1)}, u32[]{:S(2)}) copy-start(bf16[128,1,512]{2,1,0:T(2,128)(2,1)} %slice.155) | copy-start | bytes 393220
  212.6 11.2 %slice-start = ((f32[384,2,512]{2,1,0:T(2,128)}), f32[384,1,512]{2,1,0:T(1,128)S(1)}, s32[]{:S(2)}) async-start(f32[384,2,512]{2,1,0:T(2,128)} %reshape.159), calls=%async_computation.9 | async-start | bytes 1572864 | tf_op jit(solution)/shard_map/slice | solution.py:177
  212.6 11.2 %copy-start.7 = (f32[384,1,512]{2,1,0:T(1,128)S(1)}, f32[384,1,512]{2,1,0:T(1,128)}, u32[]{:S(2)}) copy-start(f32[384,1,512]{2,1,0:T(1,128)} %slice.150) | copy-start | bytes 2359300
  217.4 76.0 %all-to-all-start.4 = ((bf16[16,16,2,512]{3,1,2,0:T(8,128)(2,1)}), bf16[16,16,2,512]{3,1,2,0:T(8,128)(2,1)}, u32[]{:S(2)}, u32[]{:S(2)}) async-start(bf16[16,16,2,512]{3,1,2,0:T(8,128)(2,1)} %fusion.11), calls=%async_computation.4 | async-start | bytes 1048576 | tf_op jit(solution)/shard_map/all_to_all | solution.py:181
  223.8 1.4 copy-start.11
  (16 other events, 14.8 us)
Sparse Core Ops, SparseCore 0:
  130.5 58.9 reduce-scatter.1
  193.4 95.7 all-reduce.1
  291.6 41.7 all-gather.1
